TPU v7x, 32 devices: a whole 2x2x4 slice. The times are simulated.
32 devices in a mesh: grp: 8 (over z, x), sp: 4 (over y, core).
Axes of the slice: x: 2, y: 2, z: 4, core: 2. Of those that a mesh axis runs over, the one named last changes fastest.
Arguments:
- vis_feats: bfloat16 [2048, 1152], P('grp'), may hold values from -6 to 6
- proj_w: bfloat16 [1152, 4096], P(None, 'sp'), may hold values from -0.1875 to 0.1875
- text_embed: bfloat16 [8192, 4096], P('grp', 'sp'), may hold values from -6 to 6
- dest_group: int32 [2048], replicated, may hold values from 0 to 7, as said below
- layout: int32 [8, 1024], P('grp'), may hold values from 0 to 1023, each once within a row
- norm_gain: float32 [4096], P('sp'), may hold values from 0.1 to 1.9
- key_w: bfloat16 [4096, 512], P('sp'), may hold values from -0.09375 to 0.09375
- value_w: bfloat16 [4096, 512], P('sp'), may hold values from -0.09375 to 0.09375
Outputs:
- key_out: bfloat16 [8192, 512], P(('grp', 'sp'))
- value_out: bfloat16 [8192, 512], P(('grp', 'sp'))
Inputs may be any that keep to these rules, and one draw needn't show every extreme that they name: `dest_group`: each block of 256 rows (one encoder shard's tokens) is 4 runs of 64 consecutive rows; a run names one group, and the runs of one block name distinct groups.
All inputs are finite; a program needn't handle non-finite values.
Results may differ from a plain program's by a relative error of at most 0.024.
Values may be sent and summed in bfloat16 or wider, within the bound.
A program may use at most 64 MiB of HBM per device.

v0:
```python
import jax
import jax.numpy as jnp
from jax import lax
from jax.sharding import PartitionSpec as P

D = 4096


def local(vis_feats, proj_w, text_embed, dest_group, layout, norm_gain, key_w, value_w):
    group_count = lax.axis_size("grp")
    group_index = lax.axis_index("grp")
    seq_len = text_embed.shape[0]
    vis_dev = vis_feats.shape[0]
    run_count = group_count // 2
    capacity = vis_dev // run_count
    run_heads = dest_group.reshape(group_count, run_count, capacity)[:, :, 0]
    own_runs = lax.dynamic_index_in_dim(run_heads, group_index, 0, keepdims=False)
    raw_width = vis_feats.shape[1]
    outgoing = jnp.zeros((group_count, capacity, raw_width), jnp.bfloat16)
    outgoing = outgoing.at[own_runs].set(vis_feats.reshape(run_count, capacity, raw_width))
    incoming = lax.all_to_all(outgoing, "grp", split_axis=0, concat_axis=0, tiled=True)
    arrived = jnp.dot(
        incoming.reshape(group_count * capacity, raw_width),
        proj_w,
        preferred_element_type=jnp.float32,
    ).astype(jnp.bfloat16)
    senders = jnp.any(run_heads == group_index, axis=1).astype(jnp.int32)
    earlier = jnp.cumsum(senders) - senders
    slot_rank = earlier[:, None] * capacity + jnp.arange(capacity, dtype=jnp.int32)[None, :]
    order_row = layout[0]
    positions = jnp.where(
        senders[:, None] > 0, order_row[jnp.clip(slot_rank, 0, seq_len - 1)], seq_len
    )
    sequence = text_embed.at[positions.reshape(-1)].set(arrived, mode="drop")
    sequence_f = sequence.astype(jnp.float32)
    squares = jnp.sum(sequence_f * sequence_f, axis=1)
    scaled = (sequence_f * norm_gain).astype(jnp.bfloat16)
    kv_weight = jnp.concatenate([key_w, value_w], axis=1)
    rows_here = seq_len // lax.axis_size("sp")
    totals = lax.psum(squares, "sp")
    my_squares = lax.dynamic_slice_in_dim(totals, lax.axis_index("sp") * rows_here, rows_here, 0)
    key_value = lax.psum_scatter(
        jnp.dot(scaled, kv_weight, preferred_element_type=jnp.float32).astype(jnp.bfloat16),
        "sp",
        scatter_dimension=0,
        tiled=True,
    ).astype(jnp.float32)
    inv_rms = lax.rsqrt(my_squares / D + 1e-05)[:, None]
    key_cols = key_w.shape[1]
    key_out = (key_value[:, :key_cols] * inv_rms).astype(jnp.bfloat16)
    value_out = (key_value[:, key_cols:] * inv_rms).astype(jnp.bfloat16)
    return (key_out, value_out)


def solution(mesh):
    return jax.shard_map(
        local,
        mesh=mesh,
        in_specs=(
            P("grp", None),
            P(None, "sp"),
            P("grp", "sp"),
            P(),
            P("grp", None),
            P("sp"),
            P("sp", None),
            P("sp", None),
        ),
        out_specs=(P(("grp", "sp"), None), P(("grp", "sp"), None)),
        check_vma=False,
    )
```

profile of v0, /device:TPU:0, one launch (start us, length us, event | category | flops | bytes accessed | tf_op | source)
XLA Modules:
  0.0 104.4 jit_solution(12241986223132578177)
XLA Ops:
  7.2 0.0 copy-start
  7.2 0.0 copy-start.2
  7.2 0.0 copy-start.4
  7.2 3.3 %copy.13 = bf16[1024,1024]{1,0:T(8,128)(2,1)} copy(bf16[1024,1024]{1,0:T(8,128)(2,1)} %param.10) | data formatting | bytes 4194304
  10.5 0.0 copy-done.4
  10.5 0.1 reshape.156
  10.6 0.1 dynamic-slice_reduce_fusion
  10.7 1.2 %broadcast_in_dim.9 = bf16[8,64,1152]{2,1,0:T(8,128)(2,1)} broadcast(bf16[]{:T(256)} %constant.21.clone.1), dimensions={} | broadcast | bytes 1179650 | tf_op jit(solution)/shard_map/broadcast_in_dim | solution.py:19
  11.9 2.5 %scatter_fusion = bf16[8,64,1152]{2,1,0:T(8,128)(2,1)} fusion(bf16[8,64,1152]{2,1,0:T(8,128)(2,1)} %broadcast_in_dim.9, s32[4]{0:T(128)S(1)} %fusion.15, bf16[4,64,1152]{2,1,0:T(8,128)(2,1)S(1)} %bitcast.23), kind=kCustom, calls=%fused_computation.1 | custom fusion | bytes 1769488 | tf_op jit(solution)/shard_map/scatter | solution.py:20
  14.4 7.3 %all-to-all-start = ((bf16[8,64,1152]{2,1,0:T(8,128)(2,1)}), bf16[8,64,1152]{2,1,0:T(8,128)(2,1)S(1)}, u32[]{:S(2)}, u32[]{:S(2)}) async-start(bf16[8,64,1152]{2,1,0:T(8,128)(2,1)} %scatter_fusion), calls=%async_computation | async-start | bytes 2359296 | tf_op jit(solution)/shard_map/all_to_all | solution.py:21
  21.7 0.0 reduce-scatter.2.cloned.1.call-start
  21.8 1.0 compare_reduce_fusion
  22.7 0.5 convert_compare_fusion
  23.2 0.2 reduce-window.8
  23.4 0.1 compare_select_fusion.1
  23.5 0.1 reshape.163
  23.6 0.0 copy-done.1
  23.6 2.3 %gather_fusion = s32[512]{0:T(512)S(1)} fusion(s32[1024]{0:T(1024)S(1)} %bitcast.21, s32[1024]{0:T(1024)S(1)} %pad_clamp_fusion), kind=kCustom, calls=%fused_computation | custom fusion | bytes 6144 | tf_op jit(solution)/shard_map/gather | solution.py:32
  25.9 0.1 reshape.162
  26.0 0.1 broadcast_select_fusion
  26.1 0.1 select_n.54
  26.1 24.1 %all-to-all-done = bf16[8,64,1152]{2,1,0:T(8,128)(2,1)S(1)} async-done(((bf16[8,64,1152]{2,1,0:T(8,128)(2,1)}), bf16[8,64,1152]{2,1,0:T(8,128)(2,1)S(1)}, u32[]{:S(2)}, u32[]{:S(2)}) %all-to-all-start) | async-done | bytes 1179680 | tf_op jit(solution)/shard_map/all_to_all | solution.py:21
  50.3 2.5 %convolution_convert_fusion = bf16[512,1024]{1,0:T(8,128)(2,1)} fusion(bf16[512,1152]{1,0:T(8,128)(2,1)S(1)} %bitcast.22, bf16[1152,1024]{1,0:T(8,128)(2,1)S(1)} %copy-done), kind=kOutput, calls=%fused_computation.13 | convolution fusion | flops 1208483840 | bytes 4587520 | tf_op jit(solution)/shard_map/dot_general | solution.py:22
  52.8 6.5 %scatter_fusion.1 = bf16[1024,1024]{1,0:T(8,128)(2,1)} fusion(bf16[1024,1024]{1,0:T(8,128)(2,1)} %copy.13, s32[512]{0:T(512)S(1)} %bitcast.25, bf16[512,1024]{1,0:T(8,128)(2,1)} %convolution_convert_fusion), kind=kCustom, calls=%fused_computation.2 | custom fusion | bytes 3147776 | tf_op jit(solution)/shard_map/scatter | solution.py:34
  59.3 5.5 %fusion.8 = bf16[1024,1024]{1,0:T(8,128)(2,1)} fusion(bf16[1024,512]{1,0:T(8,128)(2,1)S(1)} %copy-done.6, bf16[1024,512]{1,0:T(8,128)(2,1)} %param.14, bf16[1024,1024]{1,0:T(8,128)(2,1)} %scatter_fusion.1, f32[1024]{0:T(1024)S(1)} %copy-done.7), kind=kOutput, calls=%fused_computation.12 | convolution fusion | flops 2155872256 | bytes 6295552 | tf_op jit(solution)/shard_map/dot_general | solution.py:43
  64.8 0.0 reduce-scatter.2.cloned.1.call-update
  64.8 2.1 %fusion.1 = f32[1024]{0:T(1024)S(1)} fusion(bf16[1024,1024]{1,0:T(8,128)(2,1)} %scatter_fusion.1), kind=kLoop, calls=%fused_computation.6 | loop fusion | flops 3144704 | bytes 2101248 | tf_op jit(solution)/shard_map/reduce_sum | solution.py:36
  66.9 5.7 %psum.7 = f32[1024]{0:T(1024)S(1)} all-reduce(f32[1024]{0:T(1024)S(1)} %fusion.1), channel_id=1, replica_groups=mesh['grp'=8,'sp'=4] {'sp'}, use_global_device_ids=true, to_apply=%region_6.7 | all-reduce | flops 1024 | bytes 8192 | tf_op jit(solution)/shard_map/psum | solution.py:40
  72.6 0.1 add_rsqrt_fusion
  72.6 22.8 %reduce-scatter.2.cloned.1.call-done = bf16[256,1024]{1,0:T(8,128)(2,1)} async-done(((bf16[1024,1024]{1,0:T(8,128)(2,1)}), bf16[256,1024]{1,0:T(8,128)(2,1)}) %reduce-scatter.2.cloned.1.call-update) | async-done | bytes 524304 | tf_op jit(solution)/shard_map/reduce_scatter | solution.py:42
  95.5 1.1 %convert_element_type.49 = f32[256,1024]{1,0:T(8,128)S(1)} convert(bf16[256,1024]{1,0:T(8,128)(2,1)} %reduce-scatter.2.cloned.1.call-done) | non-fusion elementwise | flops 262144 | bytes 1572864 | tf_op jit(solution)/shard_map/convert_element_type | solution.py:47
  96.6 0.9 fusion.13
  (15 shorter events, 0.1 us)
Async XLA Ops:
  7.2 43.1 %copy-start = (bf16[1152,1024]{1,0:T(8,128)(2,1)S(1)}, bf16[1152,1024]{1,0:T(8,128)(2,1)}, u32[]{:S(2)}) copy-start(bf16[1152,1024]{1,0:T(8,128)(2,1)} %param.9) | copy-start | bytes 7077892
  7.2 4.7 %copy-start.2 = (bf16[256,1152]{1,0:T(8,128)(2,1)S(1)}, bf16[256,1152]{1,0:T(8,128)(2,1)}, u32[]{:S(2)}) copy-start(bf16[256,1152]{1,0:T(8,128)(2,1)} %param.8) | copy-start | bytes 1769476
  7.2 3.3 %copy-start.4 = (s32[2048]{0:T(1024)S(1)}, s32[2048]{0:T(1024)}, u32[]{:S(2)}) copy-start(s32[2048]{0:T(1024)} %param.11) | copy-start | bytes 24580
  10.6 3.8 %copy-start.3 = (s32[8,4,64]{2,1,0:T(4,128)}, s32[8,4,64]{2,1,0:T(4,128)S(1)}, u32[]{:S(2)}) copy-start(s32[8,4,64]{2,1,0:T(4,128)S(1)} %reshape.156) | copy-start | bytes 24580
  11.9 11.7 %copy-start.1 = (s32[1,1024]{1,0:T(1,128)S(1)}, s32[1,1024]{1,0:T(1,128)}, u32[]{:S(2)}) copy-start(s32[1,1024]{1,0:T(1,128)} %param.12) | copy-start | bytes 12292
  14.4 35.9 %all-to-all-start = ((bf16[8,64,1152]{2,1,0:T(8,128)(2,1)}), bf16[8,64,1152]{2,1,0:T(8,128)(2,1)S(1)}, u32[]{:S(2)}, u32[]{:S(2)}) async-start(bf16[8,64,1152]{2,1,0:T(8,128)(2,1)} %scatter_fusion), calls=%async_computation | async-start | bytes 2359296 | tf_op jit(solution)/shard_map/all_to_all | solution.py:21
  21.7 73.8 %reduce-scatter.2.cloned.1.call-start = ((), (), s32[]{:S(2)}) async-start(), calls=%async_computation.2 | async-start | bytes 2621440 | tf_op jit(solution)/shard_map/reduce_scatter | solution.py:42
  23.6 2.4 %copy-start.5 = (pred[8]{0:T(512)(128)(4,1)S(1)}, pred[8]{0:T(512)(128)(4,1)}, u32[]{:S(2)}) copy-start(pred[8]{0:T(512)(128)(4,1)} %get-tuple-element.4) | copy-start | bytes 28
  52.8 6.5 %copy-start.6 = (bf16[1024,512]{1,0:T(8,128)(2,1)S(1)}, bf16[1024,512]{1,0:T(8,128)(2,1)}, u32[]{:S(2)}) copy-start(bf16[1024,512]{1,0:T(8,128)(2,1)} %param.15) | copy-start | bytes 3145732
  52.8 6.5 %copy-start.7 = (f32[1024]{0:T(1024)S(1)}, f32[1024]{0:T(1024)}, u32[]{:S(2)}) copy-start(f32[1024]{0:T(1024)} %param.13) | copy-start | bytes 12292
Sparse Core Ops, SparseCore 0:
  64.9 30.4 reduce-scatter.1
where the time goes:
time: 105 us; the launch traced here: 104 us
  waiting for transfers between devices  47 us (45%)
  local copies, waits for them, and re-layouts  16.2 us (15%)
  between operations  14.1 us (13%)
  matrix products  7.99 us (8%)
  starting transfers between devices  7.35 us (7%)
  other arithmetic  6.06 us (6%)
  blocking collectives  5.67 us (5%)
    all_to_all x1, waiting for transfers between devices, local(): lax.all_to_all(outgoing, 'grp', split_axis=0, concat_axis=0, tiled=True)  24.1 us
    reduce_scatter x1, waiting for transfers between devices, local(): lax.psum_scatter(jnp.dot(scaled, kv_weight, preferred_element_type=jnp.fl...  22.8 us
    all_to_all x1, starting transfers between devices, local(): lax.all_to_all(outgoing, 'grp', split_axis=0, concat_axis=0, tiled=True)  7.31 us
    scatter x1, local copies, waits for them, and re-layouts, local(): sequence = text_embed.at[positions.reshape(-1)].set(arrived, mode='drop')  6.5 us
    psum x1, blocking collectives, local(): totals = lax.psum(squares, 'sp')  5.67 us
    dot_general x1, matrix products, local(): jnp.dot(scaled, kv_weight, preferred_element_type=jnp.float32)  5.48 us
    unnamed x17, local copies, waits for them, and re-layouts  3.32 us
    scatter x1, local copies, waits for them, and re-layouts, local(): outgoing.at[own_runs].set(vis_feats.reshape(run_count, capacity, raw_width))  2.52 us
  transfers between devices with their start and end apart: 2, of which 2 were waited for; matrix products, arithmetic and copies ran while one was open for 6% of the time, Pallas kernels for 0%

commit v1 on v0

v1 whole, which is shorter than its diff:
```python
import functools

import jax
import jax.numpy as jnp
from jax import lax
from jax.experimental import pallas as pl
from jax.experimental.pallas import tpu as pltpu
from jax.sharding import PartitionSpec as P

EPS = 1e-05
MESH = pl.DeviceIdType.MESH
F32 = jnp.float32
BF16 = jnp.bfloat16


def as_row(column):
    return jnp.broadcast_to(column, (column.shape[0], 128)).T[:8]


def as_column(row):
    return jnp.broadcast_to(row[:1], (128, row.shape[1])).T


def kernel(
    dims,
    dest, lay, gain, vis_hbm, proj_hbm, text_hbm, key_hbm, value_hbm,
    key_out, value_out,
    vis, proj, text, weight,
    tok, tok_own, tok_send, tok_recv, tok_sq, tok_sq_recv, tok_done,
    out, ranked, onehot,
    part, core_recv, y_send, y_recv, row_sq, row_sq_recv,
    load_sem, tsq_send_sem, tsq_recv_sem, tok_send_sem, tok_recv_sem,
    out_sem, arr_sem, sq_send_sem, sq_recv_sem,
    core_send_sem, core_recv_sem, y_send_sem, y_recv_sem,
    *arrived,
):
    groups, sps, runs, cap, pad, chunks, width = dims
    ys = sps // 2
    g = lax.axis_index("grp")
    s = lax.axis_index("sp")
    y, core = s // 2, lax.rem(s, 2)
    other = 1 - core
    twin = y * 2 + other
    rows = part.shape[4]
    ranks = groups * pad
    features = text.shape[1]
    total_features = features * sps

    def load(source, target, index):
        copy = pltpu.make_async_copy(source, target, load_sem.at[index])
        copy.start()
        return copy

    load_vis = load(vis_hbm, vis, 0)
    load_proj = load(proj_hbm, proj, 1)
    load_key = load(key_hbm, weight.at[0], 2)
    load_value = load(value_hbm, weight.at[1], 3)
    load_text = load(text_hbm, text, 4)

    barrier = pltpu.get_barrier_semaphore()

    def greet_group(d, carry):
        pl.semaphore_signal(barrier, inc=1, device_id={"grp": lax.rem(g + d, groups)}, device_id_type=MESH)
        return carry

    def greet_sp(d, carry):
        pl.semaphore_signal(barrier, inc=1, device_id={"sp": lax.rem(s + d, sps)}, device_id_type=MESH)
        return carry

    lax.fori_loop(1, groups, greet_group, 0)
    lax.fori_loop(1, sps, greet_sp, 0)

    senders, earlier, count = [], [], jnp.int32(0)
    for source in range(groups):
        found = jnp.int32(0)
        for r in range(runs):
            found = found + (dest[(source * runs + r) * cap] == g).astype(jnp.int32)
        senders.append(found)
        earlier.append(count)
        count = count + found
    n_senders = count
    order = []
    for b in range(groups):
        place_of = jnp.int32(0)
        for source in range(b, groups):
            hit = senders[source] * (earlier[source] == b).astype(jnp.int32)
            place_of = place_of + hit * lax.rem(g - source + groups, groups)
        order.append(jnp.minimum(place_of, groups - 1))
    heads = [dest[(g * runs + r) * cap] for r in range(runs)]

    load_vis.wait()
    load_proj.wait()
    tile = min(256, features)

    def project(n, total):
        columns = pl.ds(pl.multiple_of(n * tile, tile), tile)
        block = jnp.dot(vis[...], proj[:, columns], preferred_element_type=F32).astype(BF16).astype(F32)
        tok[:, columns] = (block * gain[:, columns]).astype(BF16)
        return total + jnp.sum(block * block, axis=1, keepdims=True)

    squares = lax.fori_loop(0, features // tile, project, jnp.zeros((vis.shape[0], 1), F32))
    tok_sq[...] = as_row(squares)
    pl.semaphore_wait(barrier, groups - 1 + sps - 1)

    def token_square_copy(j):
        return pltpu.make_async_remote_copy(
            src_ref=tok_sq, dst_ref=tok_sq_recv.at[j],
            send_sem=tsq_send_sem.at[j], recv_sem=tsq_recv_sem.at[j],
            device_id={"sp": lax.rem(s + j, sps)}, device_id_type=MESH,
        )

    lax.fori_loop(1, sps, lambda j, c: (token_square_copy(j).start(), c)[1], 0)

    def twin_copy(k):
        return pltpu.make_async_remote_copy(
            src_ref=tok_send.at[k], dst_ref=tok_recv.at[k],
            send_sem=tok_send_sem.at[k], recv_sem=tok_recv_sem.at[k],
            device_id={"sp": twin}, device_id_type=MESH,
        )

    load_key.wait()
    load_value.wait()
    for k in range(chunks):
        columns = pl.ds(k * width, width)
        tok_send[k] = jnp.dot(tok[...], weight[other, :, columns], preferred_element_type=F32).astype(BF16)
        twin_copy(k).start()
    for k in range(chunks):
        columns = pl.ds(k * width, width)
        tok_own[k] = jnp.dot(tok[...], weight[core, :, columns], preferred_element_type=F32)

    load_text.wait()
    rank_index = lax.broadcasted_iota(jnp.int32, (1, ranks), 1)
    position_of = jnp.where(rank_index < n_senders * pad, lay[:, :ranks], -1)

    def place(q, carry):
        at = pl.ds(pl.multiple_of(q * rows, rows), rows)
        position = lax.broadcasted_iota(jnp.int32, (rows, ranks), 0) + q * rows
        hit = (position == position_of).astype(F32)
        onehot[at, :] = hit.astype(BF16)
        keep = 1.0 - jnp.max(hit, axis=1, keepdims=True)
        values = text[at, :].astype(F32)
        row_sq[q] = as_row(jnp.sum(values * values, axis=1, keepdims=True))
        text[at, :] = (values * gain[...] * keep).astype(BF16)
        return carry

    lax.fori_loop(0, sps, place, 0)

    def square_copy(j):
        partner = lax.rem(s + j, sps)
        return pltpu.make_async_remote_copy(
            src_ref=row_sq.at[partner], dst_ref=row_sq_recv.at[j],
            send_sem=sq_send_sem.at[j], recv_sem=sq_recv_sem.at[j],
            device_id={"sp": partner}, device_id_type=MESH,
        )

    lax.fori_loop(1, sps, lambda j, c: (square_copy(j).start(), c)[1], 0)

    def gather_token_squares(j, total):
        token_square_copy(j).wait()
        return total + tok_sq_recv[j]

    total = lax.fori_loop(1, sps, gather_token_squares, tok_sq[...])
    token_scale = as_column(lax.rsqrt(total / total_features + EPS))

    def group_copy(k, d):
        return pltpu.make_async_remote_copy(
            src_ref=out.at[k, d], dst_ref=arrived[k].at[d],
            send_sem=out_sem.at[k, d], recv_sem=arr_sem.at[k, d],
            device_id={"grp": lax.rem(g + d, groups)}, device_id_type=MESH,
        )

    def run_for(h):
        run = jnp.int32(0)
        for r in range(1, runs):
            run = run + r * (heads[r] == h).astype(jnp.int32)
        return jnp.minimum(run, runs - 1)

    for k in range(chunks):
        twin_copy(k).wait()
        done = ((tok_own[k] + tok_recv[k].astype(F32)) * token_scale).astype(BF16)
        tok_done[k] = done.reshape(runs, pad, width)
        arrived[k][0] = tok_done[k, run_for(g)]

        def send(d, carry):
            out[k, d] = tok_done[k, run_for(lax.rem(g + d, groups))]
            group_copy(k, d).start()
            return carry

        lax.fori_loop(1, groups, send, 0)

    def multiply(q, carry):
        at = pl.ds(pl.multiple_of(q * rows, rows), rows)
        for kind in range(2):
            product = jnp.dot(text[at, :], weight[kind], preferred_element_type=F32).astype(BF16)
            for k in range(chunks):
                part[k, lax.rem(q, 2), q // 2, kind] = product[:, k * width:(k + 1) * width]
        return carry

    lax.fori_loop(0, sps, multiply, 0)

    def core_copy(k):
        return pltpu.make_async_remote_copy(
            src_ref=part.at[k, other], dst_ref=core_recv.at[k],
            send_sem=core_send_sem.at[k], recv_sem=core_recv_sem.at[k],
            device_id={"sp": twin}, device_id_type=MESH,
        )

    def y_copy(k, j):
        return pltpu.make_async_remote_copy(
            src_ref=y_send.at[k, j], dst_ref=y_recv.at[k, j],
            send_sem=y_send_sem.at[k, j], recv_sem=y_recv_sem.at[k, j],
            device_id={"sp": lax.rem(y + j, ys) * 2 + core}, device_id_type=MESH,
        )

    def place_tokens(k, side):
        def one(yy, carry):
            at = pl.ds(pl.multiple_of((yy * 2 + side) * rows, rows), rows)
            tokens = jnp.dot(onehot[at, :], ranked[...], preferred_element_type=F32)
            part[k, side, yy, core] = (part[k, side, yy, core].astype(F32) + tokens).astype(BF16)
            return carry

        lax.fori_loop(0, ys, one, 0)

    for k in range(chunks):
        lax.fori_loop(1, groups, lambda d, c: (group_copy(k, d).wait(), c)[1], 0)

        for b in range(groups):
            ranked[b * pad:(b + 1) * pad, :] = arrived[k][order[b]]
        place_tokens(k, other)
        core_copy(k).start()
        place_tokens(k, core)
        core_copy(k).wait()

        def pass_on(j, carry):
            yy = lax.rem(y + j, ys)
            y_send[k, j] = (part[k, core, yy].astype(F32) + core_recv[k, yy].astype(F32)).astype(BF16)
            y_copy(k, j).start()
            return carry

        lax.fori_loop(1, ys, pass_on, 0)

    def gather_squares(j, total):
        square_copy(j).wait()
        return total + row_sq_recv[j]

    total = lax.fori_loop(1, sps, gather_squares, row_sq[s])
    mine = pl.ds(pl.multiple_of(s * rows, rows), rows)
    visual = jnp.max(onehot[mine, :].astype(F32), axis=1, keepdims=True)
    scale = as_column(lax.rsqrt(total / total_features + EPS))[:, :width]
    scale = jnp.where(visual > 0.5, 1.0, scale)
    for k in range(chunks):
        def add(j, sums):
            y_copy(k, j).wait()
            return sums + y_recv[k, j].astype(F32)

        sums = part[k, core, y].astype(F32) + core_recv[k, y].astype(F32)
        sums = lax.fori_loop(1, ys, add, sums)
        columns = pl.ds(k * width, width)
        key_out[:, columns] = (sums[0] * scale).astype(BF16)
        value_out[:, columns] = (sums[1] * scale).astype(BF16)


def local(groups, sps, vis_feats, proj_w, text_embed, dest_group, layout, norm_gain, key_w, value_w):
    seq_len, features = text_embed.shape
    shard, raw = vis_feats.shape
    runs = groups // 2
    cap = shard // runs
    pad = -(-cap // 16) * 16
    ranked_layout = layout
    if pad != cap:
        vis_feats = jnp.pad(vis_feats.reshape(runs, cap, raw), ((0, 0), (0, pad - cap), (0, 0)))
        vis_feats = vis_feats.reshape(runs * pad, raw)
        ranked_layout = layout[0, : groups * cap].reshape(groups, cap)
        ranked_layout = jnp.pad(ranked_layout, ((0, 0), (0, pad - cap)), constant_values=-1)
        ranked_layout = ranked_layout.reshape(1, groups * pad)
    tokens = runs * pad
    cols = key_w.shape[1]
    width = 128
    chunks = cols // width
    rows = seq_len // sps
    ys = sps // 2
    ranks = groups * pad
    dims = (groups, sps, runs, cap, pad, chunks, width)
    vmem = pl.BlockSpec(memory_space=pltpu.VMEM)
    smem = pl.BlockSpec(memory_space=pltpu.SMEM)
    anywhere = pl.BlockSpec(memory_space=pl.ANY)
    dma = pltpu.SemaphoreType.DMA
    return pl.pallas_call(
        functools.partial(kernel, dims),
        out_shape=[jax.ShapeDtypeStruct((rows, cols), BF16)] * 2,
        in_specs=[smem, vmem, vmem] + [anywhere] * 5,
        out_specs=[vmem, vmem],
        scratch_shapes=[
            pltpu.VMEM((tokens, raw), BF16),
            pltpu.VMEM((raw, features), BF16),
            pltpu.VMEM((seq_len, features), BF16),
            pltpu.VMEM((2, features, cols), BF16),
            pltpu.VMEM((tokens, features), BF16),
            pltpu.VMEM((chunks, tokens, width), F32),
            pltpu.VMEM((chunks, tokens, width), BF16),
            pltpu.VMEM((chunks, tokens, width), BF16),
            pltpu.VMEM((8, tokens), F32),
            pltpu.VMEM((sps, 8, tokens), F32),
            pltpu.VMEM((chunks, runs, pad, width), BF16),
            pltpu.VMEM((chunks, groups, pad, width), BF16),
            pltpu.VMEM((ranks, width), BF16),
            pltpu.VMEM((seq_len, ranks), BF16),
            pltpu.VMEM((chunks, 2, ys, 2, rows, width), BF16),
            pltpu.VMEM((chunks, ys, 2, rows, width), BF16),
            pltpu.VMEM((chunks, ys, 2, rows, width), BF16),
            pltpu.VMEM((chunks, ys, 2, rows, width), BF16),
            pltpu.VMEM((sps, 8, rows), F32),
            pltpu.VMEM((sps, 8, rows), F32),
            dma((5,)),
            dma((sps,)), dma((sps,)),
            dma((chunks,)), dma((chunks,)),
            dma((chunks, groups)), dma((chunks, groups)),
            dma((sps,)), dma((sps,)),
            dma((chunks,)), dma((chunks,)),
            dma((chunks, ys)), dma((chunks, ys)),
        ] + [pltpu.VMEM((groups, pad, width), BF16)] * chunks,
        compiler_params=pltpu.CompilerParams(
            collective_id=0, has_side_effects=True, vmem_limit_bytes=56 * 1024 * 1024
        ),
        cost_estimate=pl.CostEstimate(flops=5 * 10**9, bytes_accessed=8 * 2**20, transcendentals=0),
        name="route_project",
    )(dest_group, ranked_layout, norm_gain.reshape(1, features), vis_feats, proj_w, text_embed, key_w, value_w)


def solution(mesh):
    return jax.shard_map(
        functools.partial(local, mesh.shape["grp"], mesh.shape["sp"]),
        mesh=mesh,
        in_specs=(
            P("grp", None),
            P(None, "sp"),
            P("grp", "sp"),
            P(),
            P("grp", None),
            P("sp"),
            P("sp", None),
            P("sp", None),
        ),
        out_specs=(P(("grp", "sp"), None), P(("grp", "sp"), None)),
        check_vma=False,
    )
```

time: 105 us -> 39.1 us (0.37)
  waiting for transfers between devices: 47 us -> 0 us
  Pallas kernels: 0 us -> 34.9 us
  between operations: 14.1 us -> 0.64 us
  local copies, waits for them, and re-layouts: 16.2 us -> 3.34 us
  matrix products: 7.99 us -> 0 us
  starting transfers between devices: 7.35 us -> 0 us
  other arithmetic: 6.06 us -> 0 us
  blocking collectives: 5.67 us -> 0 us
    pallas_call x0 -> x1, Pallas kernels: none -> 34.9 us  [local(): pl.pallas_call(functools.partial(kernel, dims), out_shape=[jax.ShapeDtype...]
    all_to_all x1 -> x0, waiting for transfers between devices: 24.1 us -> none  [local(): lax.all_to_all(outgoing, 'grp', split_axis=0, concat_axis=0, tiled=True)]
    reduce_scatter x1 -> x0, waiting for transfers between devices: 22.8 us -> none  [local(): lax.psum_scatter(jnp.dot(scaled, kv_weight, preferred_element_type=jnp.fl...]
    scatter x2 -> x0, local copies, waits for them, and re-layouts: 9.02 us -> none  [the longest x1 6.5 us: local(): sequence = text_embed.at[positions.reshape(-1)].set(arrived, mode='drop')]
    dot_general x2 -> x0, matrix products: 7.99 us -> none  [the longest x1 5.48 us: local(): jnp.dot(scaled, kv_weight, preferred_element_type=jnp.float32)]
    all_to_all x1 -> x0, starting transfers between devices: 7.31 us -> none  [local(): lax.all_to_all(outgoing, 'grp', split_axis=0, concat_axis=0, tiled=True)]
    psum x1 -> x0, blocking collectives: 5.67 us -> none  [local(): totals = lax.psum(squares, 'sp')]
    gather x2 -> x0, local copies, waits for them, and re-layouts: 2.36 us -> none  [local(): order_row[jnp.clip(slot_rank, 0, seq_len - 1)]]
  transfers between devices with their start and end apart: 2 -> 0, of which waited for: 2 -> 0; matrix products, arithmetic and copies ran while one was open for 6% -> 0% of each run, Pallas kernels for 0% -> 0%
where the time goes in v1:
time: 39.1 us; the launch traced here: 38.9 us
  Pallas kernels  34.9 us (89%)
  local copies, waits for them, and re-layouts  3.34 us (9%)
  between operations  0.64 us (2%)
    pallas_call x1, Pallas kernels, local(): pl.pallas_call(functools.partial(kernel, dims), out_shape=[jax.ShapeDtype...  34.9 us
    unnamed x2, local copies, waits for them, and re-layouts  3.34 us

profile of v1, /device:TPU:0, one launch (start us, length us, event | category | flops | bytes accessed | tf_op | source)
XLA Modules:
  0.0 38.9 jit_solution(10706830743858066571)
XLA Ops:
  0.6 34.9 %route_project.1 = (bf16[256,512]{1,0:T(8,128)(2,1)}, bf16[256,512]{1,0:T(8,128)(2,1)}) custom-call(s32[2048]{0:T(1024)} %dest.1, s32[1,1024]{1,0:T(1,128)} %lay.1, f32[1,1024]{1,0:T(1,128)} %bitcast.1, bf16[256,1152]{1,0:T(8,128)(2,1)} %vis_hbm.1, bf16[1152,1024]{1,0:T(8,128)(2,1)} %proj_hbm.1, bf16[1024,1024]{1,0:T(8,128)(2,1)} %text_hbm.1, ...), custom_call_target="tpu_custom_call" | custom-call | flops 5000000000 | bytes 8388608 | tf_op jit(solution)/shard_map/route_project/pallas_call | solution.py:288
  35.5 1.7 %copy.12 = bf16[256,512]{1,0:T(8,128)(2,1)} copy(bf16[256,512]{1,0:T(8,128)(2,1)} %get-tuple-element.4) | data formatting | bytes 524288
  37.2 1.7 %copy.13 = bf16[256,512]{1,0:T(8,128)(2,1)} copy(bf16[256,512]{1,0:T(8,128)(2,1)} %get-tuple-element.5) | data formatting | bytes 524288

commit v2 on v1

v2 whole, which is shorter than its diff:
```python
import functools

import jax
import jax.numpy as jnp
from jax import lax
from jax.experimental import pallas as pl
from jax.experimental.pallas import tpu as pltpu
from jax.sharding import PartitionSpec as P

EPS = 1e-05
MESH = pl.DeviceIdType.MESH
F32 = jnp.float32
BF16 = jnp.bfloat16


def as_row(column):
    return jnp.broadcast_to(column, (column.shape[0], 128)).T[:8]


def as_column(row):
    return jnp.broadcast_to(row[:1], (128, row.shape[1])).T


def kernel(
    dims,
    dest, lay, gain, vis_hbm, proj_hbm, text_hbm, key_hbm, value_hbm,
    result,
    vis, proj, text, weight,
    tok, tok_own, tok_send, tok_recv, tok_y_send, tok_y_recv, tok_sq, tok_sq_recv, tok_done,
    out, ranked, onehot,
    part, core_recv, y_recv, row_sq, row_sq_recv,
    load_sem, tsq_send_sem, tsq_recv_sem, tok_send_sem, tok_recv_sem, tok_y_send_sem, tok_y_recv_sem,
    out_sem, arr_sem, sq_send_sem, sq_recv_sem,
    core_send_sem, core_recv_sem, y_send_sem, y_recv_sem,
    *arrived,
):
    groups, sps, runs, cap, pad, pieces, width = dims
    ys = sps // 2
    share = pieces * width
    g = lax.axis_index("grp")
    s = lax.axis_index("sp")
    y, core = s // 2, lax.rem(s, 2)
    other = 1 - core
    twin = y * 2 + other
    rows = part.shape[5]
    ranks = groups * pad
    features = text.shape[1]
    total_features = features * sps

    def load(source, target, index):
        copy = pltpu.make_async_copy(source, target, load_sem.at[index])
        copy.start()
        return copy

    load_vis = load(vis_hbm, vis, 0)
    load_proj = load(proj_hbm, proj, 1)
    load_key = load(key_hbm, weight.at[0], 2)
    load_value = load(value_hbm, weight.at[1], 3)
    load_text = load(text_hbm, text, 4)

    barrier = pltpu.get_barrier_semaphore()

    def greet_group(d, carry):
        pl.semaphore_signal(barrier, inc=1, device_id={"grp": lax.rem(g + d, groups)}, device_id_type=MESH)
        return carry

    def greet_sp(d, carry):
        pl.semaphore_signal(barrier, inc=1, device_id={"sp": lax.rem(s + d, sps)}, device_id_type=MESH)
        return carry

    lax.fori_loop(1, groups, greet_group, 0)
    lax.fori_loop(1, sps, greet_sp, 0)

    senders, earlier, count = [], [], jnp.int32(0)
    for source in range(groups):
        found = jnp.int32(0)
        for r in range(runs):
            found = found + (dest[(source * runs + r) * cap] == g).astype(jnp.int32)
        senders.append(found)
        earlier.append(count)
        count = count + found
    n_senders = count
    order = []
    for b in range(groups):
        place_of = jnp.int32(0)
        for source in range(b, groups):
            hit = senders[source] * (earlier[source] == b).astype(jnp.int32)
            place_of = place_of + hit * lax.rem(g - source + groups, groups)
        order.append(jnp.minimum(place_of, groups - 1))
    heads = [dest[(g * runs + r) * cap] for r in range(runs)]

    load_vis.wait()
    load_proj.wait()
    tile = min(256, features)

    def project(n, total):
        columns = pl.ds(pl.multiple_of(n * tile, tile), tile)
        block = jnp.dot(vis[...], proj[:, columns], preferred_element_type=F32).astype(BF16).astype(F32)
        tok[:, columns] = (block * gain[:, columns]).astype(BF16)
        return total + jnp.sum(block * block, axis=1, keepdims=True)

    squares = lax.fori_loop(0, features // tile, project, jnp.zeros((vis.shape[0], 1), F32))
    tok_sq[...] = as_row(squares)
    pl.semaphore_wait(barrier, groups - 1 + sps - 1)

    def token_square_copy(j):
        return pltpu.make_async_remote_copy(
            src_ref=tok_sq, dst_ref=tok_sq_recv.at[j],
            send_sem=tsq_send_sem.at[j], recv_sem=tsq_recv_sem.at[j],
            device_id={"sp": lax.rem(s + j, sps)}, device_id_type=MESH,
        )

    lax.fori_loop(1, sps, lambda j, c: (token_square_copy(j).start(), c)[1], 0)

    def twin_copy(yc):
        return pltpu.make_async_remote_copy(
            src_ref=tok_send.at[yc], dst_ref=tok_recv.at[yc],
            send_sem=tok_send_sem.at[yc], recv_sem=tok_recv_sem.at[yc],
            device_id={"sp": twin}, device_id_type=MESH,
        )

    def token_y_copy(j):
        return pltpu.make_async_remote_copy(
            src_ref=tok_y_send.at[j], dst_ref=tok_y_recv.at[j],
            send_sem=tok_y_send_sem.at[j], recv_sem=tok_y_recv_sem.at[j],
            device_id={"sp": lax.rem(y + j, ys) * 2 + core}, device_id_type=MESH,
        )

    load_key.wait()
    load_value.wait()
    product = jnp.dot(tok[...], weight[other], preferred_element_type=F32).astype(BF16)
    for yc in range(ys):
        for p in range(pieces):
            at = yc * share + p * width
            tok_send[yc, p] = product[:, at:at + width]
    lax.fori_loop(1, ys + 1, lambda j, c: (twin_copy(lax.rem(y + j, ys)).start(), c)[1], 0)
    product = jnp.dot(tok[...], weight[core], preferred_element_type=F32)
    for yc in range(ys):
        for p in range(pieces):
            at = yc * share + p * width
            tok_own[yc, p] = product[:, at:at + width]

    def pass_tokens(j, carry):
        yc = lax.rem(y + j, ys)
        twin_copy(yc).wait()
        tok_y_send[j] = (tok_own[yc] + tok_recv[yc].astype(F32)).astype(BF16)
        token_y_copy(j).start()
        return carry

    lax.fori_loop(1, ys, pass_tokens, 0)

    load_text.wait()
    rank_index = lax.broadcasted_iota(jnp.int32, (1, ranks), 1)
    position_of = jnp.where(rank_index < n_senders * pad, lay[:, :ranks], -1)

    def place(q, carry):
        at = pl.ds(pl.multiple_of(q * rows, rows), rows)
        position = lax.broadcasted_iota(jnp.int32, (rows, ranks), 0) + q * rows
        hit = (position == position_of).astype(F32)
        onehot[at, :] = hit.astype(BF16)
        keep = 1.0 - jnp.max(hit, axis=1, keepdims=True)
        values = text[at, :].astype(F32)
        row_sq[q] = as_row(jnp.sum(values * values, axis=1, keepdims=True))
        text[at, :] = (values * gain[...] * keep).astype(BF16)
        return carry

    lax.fori_loop(0, sps, place, 0)

    def square_copy(j):
        partner = lax.rem(s + j, sps)
        return pltpu.make_async_remote_copy(
            src_ref=row_sq.at[partner], dst_ref=row_sq_recv.at[j],
            send_sem=sq_send_sem.at[j], recv_sem=sq_recv_sem.at[j],
            device_id={"sp": partner}, device_id_type=MESH,
        )

    lax.fori_loop(1, sps, lambda j, c: (square_copy(j).start(), c)[1], 0)

    def multiply_share(yc):
        columns = pl.ds(pl.multiple_of(yc * share, share), share)

        def one(q, carry):
            at = pl.ds(pl.multiple_of(q * rows, rows), rows)
            for kind in range(2):
                block = jnp.dot(text[at, :], weight[kind, :, columns], preferred_element_type=F32).astype(BF16)
                for p in range(pieces):
                    part[yc, p, lax.rem(q, 2), q // 2, kind] = block[:, p * width:(p + 1) * width]
            return carry

        lax.fori_loop(0, sps, one, 0)

    def multiply_all(q, carry):
        at = pl.ds(pl.multiple_of(q * rows, rows), rows)
        for kind in range(2):
            block = jnp.dot(text[at, :], weight[kind], preferred_element_type=F32).astype(BF16)
            for yc in range(ys):
                for p in range(pieces):
                    first = yc * share + p * width
                    part[yc, p, lax.rem(q, 2), q // 2, kind] = block[:, first:first + width]
        return carry

    def core_copy(yc, p):
        return pltpu.make_async_remote_copy(
            src_ref=part.at[yc, p, other], dst_ref=core_recv.at[yc, p],
            send_sem=core_send_sem.at[yc, p], recv_sem=core_recv_sem.at[yc, p],
            device_id={"sp": twin}, device_id_type=MESH,
        )

    def y_copy(yc, p, j):
        yy = lax.rem(y + j, ys)
        return pltpu.make_async_remote_copy(
            src_ref=part.at[yc, p, core, yy], dst_ref=y_recv.at[yc, p, j],
            send_sem=y_send_sem.at[yc, p, j], recv_sem=y_recv_sem.at[yc, p, j],
            device_id={"sp": yy * 2 + core}, device_id_type=MESH,
        )

    def pass_on(yc, p):
        core_copy(yc, p).wait()

        def one(j, carry):
            yy = lax.rem(y + j, ys)
            pair = part[yc, p, core, yy].astype(F32) + core_recv[yc, p, yy].astype(F32)
            part[yc, p, core, yy] = pair.astype(BF16)
            y_copy(yc, p, j).start()
            return carry

        lax.fori_loop(1, ys, one, 0)

    by_share = share % 128 == 0
    if not by_share:
        lax.fori_loop(0, sps, multiply_all, 0)

    def other_share(j, carry):
        yc = lax.rem(y + j, ys)
        if by_share:
            multiply_share(yc)
        for p in range(pieces):
            core_copy(yc, p).start()
        return carry

    lax.fori_loop(1, ys, other_share, 0)

    def gather_token_squares(j, total):
        token_square_copy(j).wait()
        return total + tok_sq_recv[j]

    total = lax.fori_loop(1, sps, gather_token_squares, tok_sq[...])
    token_scale = as_column(lax.rsqrt(total / total_features + EPS))[:, :width]

    def group_copy(p, d):
        return pltpu.make_async_remote_copy(
            src_ref=out.at[p, d], dst_ref=arrived[p].at[d],
            send_sem=out_sem.at[p, d], recv_sem=arr_sem.at[p, d],
            device_id={"grp": lax.rem(g + d, groups)}, device_id_type=MESH,
        )

    def run_for(h):
        run = jnp.int32(0)
        for r in range(1, runs):
            run = run + r * (heads[r] == h).astype(jnp.int32)
        return jnp.minimum(run, runs - 1)

    def gather_tokens(j, sums):
        token_y_copy(j).wait()
        return sums + tok_y_recv[j].astype(F32)

    twin_copy(y).wait()
    sums = lax.fori_loop(1, ys, gather_tokens, tok_own[y] + tok_recv[y].astype(F32))
    for p in range(pieces):
        tok_done[p] = (sums[p] * token_scale).astype(BF16).reshape(runs, pad, width)
        arrived[p][0] = tok_done[p, run_for(g)]

        def send(d, carry):
            out[p, d] = tok_done[p, run_for(lax.rem(g + d, groups))]
            group_copy(p, d).start()
            return carry

        lax.fori_loop(1, groups, send, 0)

    def other_pass(j, carry):
        for p in range(pieces):
            pass_on(lax.rem(y + j, ys), p)
        return carry

    lax.fori_loop(1, ys, other_pass, 0)

    if by_share:
        multiply_share(y)

    def place_tokens(p, side):
        def one(yy, carry):
            at = pl.ds(pl.multiple_of((yy * 2 + side) * rows, rows), rows)
            tokens = jnp.dot(onehot[at, :], ranked[...], preferred_element_type=F32)
            part[y, p, side, yy, core] = (part[y, p, side, yy, core].astype(F32) + tokens).astype(BF16)
            return carry

        lax.fori_loop(0, ys, one, 0)

    for p in range(pieces):
        lax.fori_loop(1, groups, lambda d, c: (group_copy(p, d).wait(), c)[1], 0)
        for b in range(groups):
            ranked[b * pad:(b + 1) * pad, :] = arrived[p][order[b]]
        place_tokens(p, other)
        core_copy(y, p).start()
        place_tokens(p, core)
        pass_on(y, p)

    def gather_squares(j, total):
        square_copy(j).wait()
        return total + row_sq_recv[j]

    total = lax.fori_loop(1, sps, gather_squares, row_sq[s])
    mine = pl.ds(pl.multiple_of(s * rows, rows), rows)
    visual = jnp.max(onehot[mine, :].astype(F32), axis=1, keepdims=True)
    scale = as_column(lax.rsqrt(total / total_features + EPS))[:, :width]
    scale = jnp.where(visual > 0.5, 1.0, scale)
    for p in range(pieces):
        for yc in range(ys):
            def add(j, sums):
                y_copy(yc, p, j).wait()
                return sums + y_recv[yc, p, j].astype(F32)

            sums = part[yc, p, core, y].astype(F32) + core_recv[yc, p, y].astype(F32)
            sums = lax.fori_loop(1, ys, add, sums)
            first = yc * share + p * width
            result[0, :, first:first + width] = (sums[0] * scale).astype(BF16)
            result[1, :, first:first + width] = (sums[1] * scale).astype(BF16)


def split(both, key_out, value_out, sem):
    copies = [pltpu.make_async_copy(both.at[i], target, sem.at[i]) for i, target in enumerate((key_out, value_out))]
    for copy in copies:
        copy.start()
    for copy in copies:
        copy.wait()


def local(groups, sps, vis_feats, proj_w, text_embed, dest_group, layout, norm_gain, key_w, value_w):
    seq_len, features = text_embed.shape
    shard, raw = vis_feats.shape
    runs = groups // 2
    cap = shard // runs
    pad = -(-cap // 16) * 16
    ranked_layout = layout
    if pad != cap:
        vis_feats = jnp.pad(vis_feats.reshape(runs, cap, raw), ((0, 0), (0, pad - cap), (0, 0)))
        vis_feats = vis_feats.reshape(runs * pad, raw)
        ranked_layout = layout[0, : groups * cap].reshape(groups, cap)
        ranked_layout = jnp.pad(ranked_layout, ((0, 0), (0, pad - cap)), constant_values=-1)
        ranked_layout = ranked_layout.reshape(1, groups * pad)
    tokens = runs * pad
    cols = key_w.shape[1]
    rows = seq_len // sps
    ys = sps // 2
    width = min(128, cols // ys)
    pieces = cols // (ys * width)
    ranks = groups * pad
    dims = (groups, sps, runs, cap, pad, pieces, width)
    vmem = pl.BlockSpec(memory_space=pltpu.VMEM)
    smem = pl.BlockSpec(memory_space=pltpu.SMEM)
    anywhere = pl.BlockSpec(memory_space=pl.ANY)
    dma = pltpu.SemaphoreType.DMA
    both = pl.pallas_call(
        functools.partial(kernel, dims),
        out_shape=jax.ShapeDtypeStruct((2, rows, cols), BF16),
        in_specs=[smem, vmem, vmem] + [anywhere] * 5,
        out_specs=vmem,
        scratch_shapes=[
            pltpu.VMEM((tokens, raw), BF16),
            pltpu.VMEM((raw, features), BF16),
            pltpu.VMEM((seq_len, features), BF16),
            pltpu.VMEM((2, features, cols), BF16),
            pltpu.VMEM((tokens, features), BF16),
            pltpu.VMEM((ys, pieces, tokens, width), F32),
            pltpu.VMEM((ys, pieces, tokens, width), BF16),
            pltpu.VMEM((ys, pieces, tokens, width), BF16),
            pltpu.VMEM((ys, pieces, tokens, width), BF16),
            pltpu.VMEM((ys, pieces, tokens, width), BF16),
            pltpu.VMEM((8, tokens), F32),
            pltpu.VMEM((sps, 8, tokens), F32),
            pltpu.VMEM((pieces, runs, pad, width), BF16),
            pltpu.VMEM((pieces, groups, pad, width), BF16),
            pltpu.VMEM((ranks, width), BF16),
            pltpu.VMEM((seq_len, ranks), BF16),
            pltpu.VMEM((ys, pieces, 2, ys, 2, rows, width), BF16),
            pltpu.VMEM((ys, pieces, ys, 2, rows, width), BF16),
            pltpu.VMEM((ys, pieces, ys, 2, rows, width), BF16),
            pltpu.VMEM((sps, 8, rows), F32),
            pltpu.VMEM((sps, 8, rows), F32),
            dma((5,)),
            dma((sps,)), dma((sps,)),
            dma((ys,)), dma((ys,)), dma((ys,)), dma((ys,)),
            dma((pieces, groups)), dma((pieces, groups)),
            dma((sps,)), dma((sps,)),
            dma((ys, pieces)), dma((ys, pieces)),
            dma((ys, pieces, ys)), dma((ys, pieces, ys)),
        ] + [pltpu.VMEM((groups, pad, width), BF16)] * pieces,
        compiler_params=pltpu.CompilerParams(
            collective_id=0, has_side_effects=True, vmem_limit_bytes=60 * 1024 * 1024
        ),
        cost_estimate=pl.CostEstimate(flops=5 * 10**9, bytes_accessed=8 * 2**20, transcendentals=0),
        name="route_project",
    )(dest_group, ranked_layout, norm_gain.reshape(1, features), vis_feats, proj_w, text_embed, key_w, value_w)
    return pl.pallas_call(
        split,
        out_shape=[jax.ShapeDtypeStruct((rows, cols), BF16)] * 2,
        in_specs=[anywhere],
        out_specs=[anywhere, anywhere],
        scratch_shapes=[dma((2,))],
        compiler_params=pltpu.CompilerParams(vmem_limit_bytes=60 * 1024 * 1024),
        name="split_result",
    )(both)


def solution(mesh):
    return jax.shard_map(
        functools.partial(local, mesh.shape["grp"], mesh.shape["sp"]),
        mesh=mesh,
        in_specs=(
            P("grp", None),
            P(None, "sp"),
            P("grp", "sp"),
            P(),
            P("grp", None),
            P("sp"),
            P("sp", None),
            P("sp", None),
        ),
        out_specs=(P(("grp", "sp"), None), P(("grp", "sp"), None)),
        check_vma=False,
    )
```

time: 39.1 us -> 49.1 us (1.26)
  Pallas kernels: 34.9 us -> 48.2 us
  local copies, waits for them, and re-layouts: 3.34 us -> 0 us
    pallas_call x1 -> x2, Pallas kernels: 34.9 us -> 48.2 us  [the longest x1 31.2 us: local(): pl.pallas_call(functools.partial(kernel, dims), out_shape=jax.ShapeDtypeS...]
    unnamed x2 -> x0, local copies, waits for them, and re-layouts: 3.34 us -> none
where the time goes in v2:
time: 49.1 us; the launch traced here: 48.9 us
  Pallas kernels  48.2 us (98%)
  between operations  0.64 us (1%)
    pallas_call x1, Pallas kernels, local(): pl.pallas_call(functools.partial(kernel, dims), out_shape=jax.ShapeDtypeS...  31.2 us
    pallas_call x1, Pallas kernels, local(): pl.pallas_call(split, out_shape=[jax.ShapeDtypeStruct((rows, cols), BF16)...  17 us

profile of v2, /device:TPU:0, one launch (start us, length us, event | category | flops | bytes accessed | tf_op | source)
XLA Modules:
  0.0 48.9 jit_solution(7051231001055359382)
XLA Ops:
  0.6 31.2 %route_project.1.both = bf16[2,256,512]{2,1,0:T(8,128)(2,1)} custom-call(s32[2048]{0:T(1024)} %dest.1, s32[1,1024]{1,0:T(1,128)} %lay.1, f32[1,1024]{1,0:T(1,128)} %bitcast.1, bf16[256,1152]{1,0:T(8,128)(2,1)} %vis_hbm.1, bf16[1152,1024]{1,0:T(8,128)(2,1)} %proj_hbm.1, bf16[1024,1024]{1,0:T(8,128)(2,1)} %text_hbm.1, bf16[1024,512]{1,0:T(8,128)(2,1)} %key_hbm.1, ...), custom_call_target="tpu_custom_call" | custom-call | flops 5000000000 | bytes 8388608 | tf_op jit(solution)/shard_map/route_project/pallas_call | solution.py:363
  31.9 17.0 %split_result.1 = (bf16[256,512]{1,0:T(8,128)(2,1)}, bf16[256,512]{1,0:T(8,128)(2,1)}) custom-call(bf16[2,256,512]{2,1,0:T(8,128)(2,1)} %route_project.1.both), custom_call_target="tpu_custom_call" | custom-call | tf_op jit(solution)/shard_map/split_result/pallas_call | solution.py:404

commit v3 on v2

--- a/solution.py
+++ b/solution.py
@@ -29,7 +29,7 @@
     tok, tok_own, tok_send, tok_recv, tok_y_send, tok_y_recv, tok_sq, tok_sq_recv, tok_done,
     out, ranked, onehot,
     part, core_recv, y_recv, row_sq, row_sq_recv,
-    load_sem, tsq_send_sem, tsq_recv_sem, tok_send_sem, tok_recv_sem, tok_y_send_sem, tok_y_recv_sem,
+    load_sem, proj_sem, tsq_send_sem, tsq_recv_sem, tok_send_sem, tok_recv_sem, tok_y_send_sem, tok_y_recv_sem,
     out_sem, arr_sem, sq_send_sem, sq_recv_sem,
     core_send_sem, core_recv_sem, y_send_sem, y_recv_sem,
     *arrived,
@@ -52,11 +52,18 @@
         copy.start()
         return copy
 
+    tile = min(256, features)
+
+    def proj_copy(n):
+        columns = pl.ds(pl.multiple_of(n * tile, tile), tile)
+        return pltpu.make_async_copy(proj_hbm.at[:, columns], proj.at[:, columns], proj_sem.at[n])
+
     load_vis = load(vis_hbm, vis, 0)
-    load_proj = load(proj_hbm, proj, 1)
-    load_key = load(key_hbm, weight.at[0], 2)
-    load_value = load(value_hbm, weight.at[1], 3)
-    load_text = load(text_hbm, text, 4)
+    for n in range(features // tile):
+        proj_copy(n).start()
+    load_key = load(key_hbm, weight.at[0], 1)
+    load_value = load(value_hbm, weight.at[1], 2)
+    load_text = load(text_hbm, text, 3)
 
     barrier = pltpu.get_barrier_semaphore()
 
@@ -90,10 +97,9 @@
     heads = [dest[(g * runs + r) * cap] for r in range(runs)]
 
     load_vis.wait()
-    load_proj.wait()
-    tile = min(256, features)
 
     def project(n, total):
+        proj_copy(n).wait()
         columns = pl.ds(pl.multiple_of(n * tile, tile), tile)
         block = jnp.dot(vis[...], proj[:, columns], preferred_element_type=F32).astype(BF16).astype(F32)
         tok[:, columns] = (block * gain[:, columns]).astype(BF16)
@@ -119,10 +125,10 @@
             device_id={"sp": twin}, device_id_type=MESH,
         )
 
-    def token_y_copy(j):
-        return pltpu.make_async_remote_copy(
-            src_ref=tok_y_send.at[j], dst_ref=tok_y_recv.at[j],
-            send_sem=tok_y_send_sem.at[j], recv_sem=tok_y_recv_sem.at[j],
+    def token_y_copy(j, p):
+        return pltpu.make_async_remote_copy(
+            src_ref=tok_y_send.at[j, p], dst_ref=tok_y_recv.at[j, p],
+            send_sem=tok_y_send_sem.at[j, p], recv_sem=tok_y_recv_sem.at[j, p],
             device_id={"sp": lax.rem(y + j, ys) * 2 + core}, device_id_type=MESH,
         )
 
@@ -143,8 +149,9 @@
     def pass_tokens(j, carry):
         yc = lax.rem(y + j, ys)
         twin_copy(yc).wait()
-        tok_y_send[j] = (tok_own[yc] + tok_recv[yc].astype(F32)).astype(BF16)
-        token_y_copy(j).start()
+        for p in range(pieces):
+            tok_y_send[j, p] = (tok_own[yc, p] + tok_recv[yc, p].astype(F32)).astype(BF16)
+            token_y_copy(j, p).start()
         return carry
 
     lax.fori_loop(1, ys, pass_tokens, 0)
@@ -153,7 +160,7 @@
     rank_index = lax.broadcasted_iota(jnp.int32, (1, ranks), 1)
     position_of = jnp.where(rank_index < n_senders * pad, lay[:, :ranks], -1)
 
-    def place(q, carry):
+    def place(q):
         at = pl.ds(pl.multiple_of(q * rows, rows), rows)
         position = lax.broadcasted_iota(jnp.int32, (rows, ranks), 0) + q * rows
         hit = (position == position_of).astype(F32)
@@ -162,9 +169,6 @@
         values = text[at, :].astype(F32)
         row_sq[q] = as_row(jnp.sum(values * values, axis=1, keepdims=True))
         text[at, :] = (values * gain[...] * keep).astype(BF16)
-        return carry
-
-    lax.fori_loop(0, sps, place, 0)
 
     def square_copy(j):
         partner = lax.rem(s + j, sps)
@@ -174,22 +178,17 @@
             device_id={"sp": partner}, device_id_type=MESH,
         )
 
-    lax.fori_loop(1, sps, lambda j, c: (square_copy(j).start(), c)[1], 0)
-
-    def multiply_share(yc):
+    by_share = share % 128 == 0
+
+    def multiply(q, yc):
+        at = pl.ds(pl.multiple_of(q * rows, rows), rows)
         columns = pl.ds(pl.multiple_of(yc * share, share), share)
-
-        def one(q, carry):
-            at = pl.ds(pl.multiple_of(q * rows, rows), rows)
-            for kind in range(2):
-                block = jnp.dot(text[at, :], weight[kind, :, columns], preferred_element_type=F32).astype(BF16)
-                for p in range(pieces):
-                    part[yc, p, lax.rem(q, 2), q // 2, kind] = block[:, p * width:(p + 1) * width]
-            return carry
-
-        lax.fori_loop(0, sps, one, 0)
-
-    def multiply_all(q, carry):
+        for kind in range(2):
+            block = jnp.dot(text[at, :], weight[kind, :, columns], preferred_element_type=F32).astype(BF16)
+            for p in range(pieces):
+                part[yc, p, lax.rem(q, 2), q // 2, kind] = block[:, p * width:(p + 1) * width]
+
+    def multiply_all(q):
         at = pl.ds(pl.multiple_of(q * rows, rows), rows)
         for kind in range(2):
             block = jnp.dot(text[at, :], weight[kind], preferred_element_type=F32).astype(BF16)
@@ -197,12 +196,11 @@
                 for p in range(pieces):
                     first = yc * share + p * width
                     part[yc, p, lax.rem(q, 2), q // 2, kind] = block[:, first:first + width]
-        return carry
-
-    def core_copy(yc, p):
-        return pltpu.make_async_remote_copy(
-            src_ref=part.at[yc, p, other], dst_ref=core_recv.at[yc, p],
-            send_sem=core_send_sem.at[yc, p], recv_sem=core_recv_sem.at[yc, p],
+
+    def core_copy(yc, p, yy):
+        return pltpu.make_async_remote_copy(
+            src_ref=part.at[yc, p, other, yy], dst_ref=core_recv.at[yc, p, yy],
+            send_sem=core_send_sem.at[yc, p, yy], recv_sem=core_recv_sem.at[yc, p, yy],
             device_id={"sp": twin}, device_id_type=MESH,
         )
 
@@ -215,10 +213,9 @@
         )
 
     def pass_on(yc, p):
-        core_copy(yc, p).wait()
-
         def one(j, carry):
             yy = lax.rem(y + j, ys)
+            core_copy(yc, p, yy).wait()
             pair = part[yc, p, core, yy].astype(F32) + core_recv[yc, p, yy].astype(F32)
             part[yc, p, core, yy] = pair.astype(BF16)
             y_copy(yc, p, j).start()
@@ -226,19 +223,26 @@
 
         lax.fori_loop(1, ys, one, 0)
 
-    by_share = share % 128 == 0
-    if not by_share:
-        lax.fori_loop(0, sps, multiply_all, 0)
-
-    def other_share(j, carry):
-        yc = lax.rem(y + j, ys)
-        if by_share:
-            multiply_share(yc)
-        for p in range(pieces):
-            core_copy(yc, p).start()
-        return carry
-
-    lax.fori_loop(1, ys, other_share, 0)
+    def prepare(yy):
+        def one(side, carry):
+            q = yy * 2 + side
+            place(q)
+            if by_share:
+                lax.fori_loop(1, ys, lambda j, c: (multiply(q, lax.rem(y + j, ys)), c)[1], 0)
+            else:
+                multiply_all(q)
+            return carry
+
+        lax.fori_loop(0, 2, one, 0)
+
+        def send_share(j, carry):
+            for p in range(pieces):
+                core_copy(lax.rem(y + j, ys), p, yy).start()
+            return carry
+
+        lax.fori_loop(1, ys, send_share, 0)
+
+    lax.fori_loop(1, ys, lambda j, c: (prepare(lax.rem(y + j, ys)), c)[1], 0)
 
     def gather_token_squares(j, total):
         token_square_copy(j).wait()
@@ -260,14 +264,14 @@
             run = run + r * (heads[r] == h).astype(jnp.int32)
         return jnp.minimum(run, runs - 1)
 
-    def gather_tokens(j, sums):
-        token_y_copy(j).wait()
-        return sums + tok_y_recv[j].astype(F32)
-
     twin_copy(y).wait()
-    sums = lax.fori_loop(1, ys, gather_tokens, tok_own[y] + tok_recv[y].astype(F32))
     for p in range(pieces):
-        tok_done[p] = (sums[p] * token_scale).astype(BF16).reshape(runs, pad, width)
+        def gather_tokens(j, sums):
+            token_y_copy(j, p).wait()
+            return sums + tok_y_recv[j, p].astype(F32)
+
+        sums = lax.fori_loop(1, ys, gather_tokens, tok_own[y, p] + tok_recv[y, p].astype(F32))
+        tok_done[p] = (sums * token_scale).astype(BF16).reshape(runs, pad, width)
         arrived[p][0] = tok_done[p, run_for(g)]
 
         def send(d, carry):
@@ -276,33 +280,32 @@
             return carry
 
         lax.fori_loop(1, groups, send, 0)
-
-    def other_pass(j, carry):
-        for p in range(pieces):
-            pass_on(lax.rem(y + j, ys), p)
-        return carry
-
-    lax.fori_loop(1, ys, other_pass, 0)
+        lax.fori_loop(1, ys, lambda j, c: (pass_on(lax.rem(y + j, ys), p), c)[1], 0)
+
+    prepare(y)
+    lax.fori_loop(1, sps, lambda j, c: (square_copy(j).start(), c)[1], 0)
 
     if by_share:
-        multiply_share(y)
-
-    def place_tokens(p, side):
-        def one(yy, carry):
-            at = pl.ds(pl.multiple_of((yy * 2 + side) * rows, rows), rows)
-            tokens = jnp.dot(onehot[at, :], ranked[...], preferred_element_type=F32)
-            part[y, p, side, yy, core] = (part[y, p, side, yy, core].astype(F32) + tokens).astype(BF16)
-            return carry
-
-        lax.fori_loop(0, ys, one, 0)
+        lax.fori_loop(0, sps, lambda q, c: (multiply(q, y), c)[1], 0)
+
+    def place_tokens(p, side, yy):
+        at = pl.ds(pl.multiple_of((yy * 2 + side) * rows, rows), rows)
+        tokens = jnp.dot(onehot[at, :], ranked[...], preferred_element_type=F32)
+        part[y, p, side, yy, core] = (part[y, p, side, yy, core].astype(F32) + tokens).astype(BF16)
 
     for p in range(pieces):
         lax.fori_loop(1, groups, lambda d, c: (group_copy(p, d).wait(), c)[1], 0)
         for b in range(groups):
             ranked[b * pad:(b + 1) * pad, :] = arrived[p][order[b]]
-        place_tokens(p, other)
-        core_copy(y, p).start()
-        place_tokens(p, core)
+
+        def place_and_send(j, carry):
+            yy = lax.rem(y + j, ys)
+            place_tokens(p, other, yy)
+            core_copy(y, p, yy).start()
+            return carry
+
+        lax.fori_loop(1, ys + 1, place_and_send, 0)
+        lax.fori_loop(1, ys + 1, lambda j, c: (place_tokens(p, core, lax.rem(y + j, ys)), c)[1], 0)
         pass_on(y, p)
 
     def gather_squares(j, total):
@@ -320,6 +323,7 @@
                 y_copy(yc, p, j).wait()
                 return sums + y_recv[yc, p, j].astype(F32)
 
+            core_copy(yc, p, y).wait()
             sums = part[yc, p, core, y].astype(F32) + core_recv[yc, p, y].astype(F32)
             sums = lax.fori_loop(1, ys, add, sums)
             first = yc * share + p * width
@@ -327,12 +331,16 @@
             result[1, :, first:first + width] = (sums[1] * scale).astype(BF16)
 
 
-def split(both, key_out, value_out, sem):
-    copies = [pltpu.make_async_copy(both.at[i], target, sem.at[i]) for i, target in enumerate((key_out, value_out))]
-    for copy in copies:
+def split(both, key_out, value_out, held, in_sem, out_sem):
+    loads = [pltpu.make_async_copy(both.at[i], held.at[i], in_sem.at[i]) for i in range(2)]
+    stores = [pltpu.make_async_copy(held.at[i], to, out_sem.at[i]) for i, to in enumerate((key_out, value_out))]
+    for copy in loads:
         copy.start()
-    for copy in copies:
+    for copy, store in zip(loads, stores):
         copy.wait()
+        store.start()
+    for store in stores:
+        store.wait()
 
 
 def local(groups, sps, vis_feats, proj_w, text_embed, dest_group, layout, norm_gain, key_w, value_w):
@@ -387,12 +395,12 @@
             pltpu.VMEM((ys, pieces, ys, 2, rows, width), BF16),
             pltpu.VMEM((sps, 8, rows), F32),
             pltpu.VMEM((sps, 8, rows), F32),
-            dma((5,)),
+            dma((4,)), dma((features // min(256, features),)),
             dma((sps,)), dma((sps,)),
-            dma((ys,)), dma((ys,)), dma((ys,)), dma((ys,)),
+            dma((ys,)), dma((ys,)), dma((ys, pieces)), dma((ys, pieces)),
             dma((pieces, groups)), dma((pieces, groups)),
             dma((sps,)), dma((sps,)),
-            dma((ys, pieces)), dma((ys, pieces)),
+            dma((ys, pieces, ys)), dma((ys, pieces, ys)),
             dma((ys, pieces, ys)), dma((ys, pieces, ys)),
         ] + [pltpu.VMEM((groups, pad, width), BF16)] * pieces,
         compiler_params=pltpu.CompilerParams(
@@ -406,7 +414,7 @@
         out_shape=[jax.ShapeDtypeStruct((rows, cols), BF16)] * 2,
         in_specs=[anywhere],
         out_specs=[anywhere, anywhere],
-        scratch_shapes=[dma((2,))],
+        scratch_shapes=[pltpu.VMEM((2, rows, cols), BF16), dma((2,)), dma((2,))],
         compiler_params=pltpu.CompilerParams(vmem_limit_bytes=60 * 1024 * 1024),
         name="split_result",
     )(both)

time: 49.1 us -> 30.6 us (0.62)
  Pallas kernels: 48.2 us -> 29.7 us
    pallas_call x1, Pallas kernels: 17 us -> 1.77 us  [local(): pl.pallas_call(split, out_shape=[jax.ShapeDtypeStruct((rows, cols), BF16)...]
    pallas_call x1, Pallas kernels: 31.2 us -> 27.9 us  [local(): pl.pallas_call(functools.partial(kernel, dims), out_shape=jax.ShapeDtypeS...]
where the time goes in v3:
time: 30.6 us; the launch traced here: 30.4 us
  Pallas kernels  29.7 us (97%)
  between operations  0.64 us (2%)
    pallas_call x1, Pallas kernels, local(): pl.pallas_call(functools.partial(kernel, dims), out_shape=jax.ShapeDtypeS...  27.9 us
    pallas_call x1, Pallas kernels, local(): pl.pallas_call(split, out_shape=[jax.ShapeDtypeStruct((rows, cols), BF16)...  1.77 us

profile of v3, /device:TPU:0, one launch (start us, length us, event | category | flops | bytes accessed | tf_op | source)
XLA Modules:
  0.0 30.4 jit_solution(11255633338209594844)
XLA Ops:
  0.6 27.9 %route_project.1.both = bf16[2,256,512]{2,1,0:T(8,128)(2,1)} custom-call(s32[2048]{0:T(1024)} %dest.1, s32[1,1024]{1,0:T(1,128)} %lay.1, f32[1,1024]{1,0:T(1,128)} %bitcast.1, bf16[256,1152]{1,0:T(8,128)(2,1)} %vis_hbm.1, bf16[1152,1024]{1,0:T(8,128)(2,1)} %proj_hbm.1, bf16[1024,1024]{1,0:T(8,128)(2,1)} %text_hbm.1, bf16[1024,512]{1,0:T(8,128)(2,1)} %key_hbm.1, ...), custom_call_target="tpu_custom_call" | custom-call | flops 5000000000 | bytes 8388608 | tf_op jit(solution)/shard_map/route_project/pallas_call | solution.py:371
  28.6 1.8 %split_result.1 = (bf16[256,512]{1,0:T(8,128)(2,1)}, bf16[256,512]{1,0:T(8,128)(2,1)}) custom-call(bf16[2,256,512]{2,1,0:T(8,128)(2,1)} %route_project.1.both), custom_call_target="tpu_custom_call" | custom-call | tf_op jit(solution)/shard_map/split_result/pallas_call | solution.py:412

commit v4 on v3

--- a/solution.py
+++ b/solution.py
@@ -31,7 +31,7 @@
     part, core_recv, y_recv, row_sq, row_sq_recv,
     load_sem, proj_sem, tsq_send_sem, tsq_recv_sem, tok_send_sem, tok_recv_sem, tok_y_send_sem, tok_y_recv_sem,
     out_sem, arr_sem, sq_send_sem, sq_recv_sem,
-    core_send_sem, core_recv_sem, y_send_sem, y_recv_sem,
+    core_send_sem, core_recv_sem, y_send_sem, y_recv_sem, held, result_sem,
     *arrived,
 ):
     groups, sps, runs, cap, pad, pieces, width = dims
@@ -63,7 +63,6 @@
         proj_copy(n).start()
     load_key = load(key_hbm, weight.at[0], 1)
     load_value = load(value_hbm, weight.at[1], 2)
-    load_text = load(text_hbm, text, 3)
 
     barrier = pltpu.get_barrier_semaphore()
 
@@ -98,14 +97,15 @@
 
     load_vis.wait()
 
-    def project(n, total):
+    squares = jnp.zeros((vis.shape[0], 1), F32)
+    for n in range(features // tile):
         proj_copy(n).wait()
-        columns = pl.ds(pl.multiple_of(n * tile, tile), tile)
+        if n == 0:
+            load_text = load(text_hbm, text, 3)
+        columns = pl.ds(n * tile, tile)
         block = jnp.dot(vis[...], proj[:, columns], preferred_element_type=F32).astype(BF16).astype(F32)
         tok[:, columns] = (block * gain[:, columns]).astype(BF16)
-        return total + jnp.sum(block * block, axis=1, keepdims=True)
-
-    squares = lax.fori_loop(0, features // tile, project, jnp.zeros((vis.shape[0], 1), F32))
+        squares = squares + jnp.sum(block * block, axis=1, keepdims=True)
     tok_sq[...] = as_row(squares)
     pl.semaphore_wait(barrier, groups - 1 + sps - 1)
 
@@ -224,16 +224,15 @@
         lax.fori_loop(1, ys, one, 0)
 
     def prepare(yy):
-        def one(side, carry):
+        for side in range(2):
             q = yy * 2 + side
             place(q)
-            if by_share:
+            if not by_share:
+                multiply_all(q)
+            elif ys == 2:
+                multiply(q, 1 - y)
+            else:
                 lax.fori_loop(1, ys, lambda j, c: (multiply(q, lax.rem(y + j, ys)), c)[1], 0)
-            else:
-                multiply_all(q)
-            return carry
-
-        lax.fori_loop(0, 2, one, 0)
 
         def send_share(j, carry):
             for p in range(pieces):
@@ -286,7 +285,17 @@
     lax.fori_loop(1, sps, lambda j, c: (square_copy(j).start(), c)[1], 0)
 
     if by_share:
-        lax.fori_loop(0, sps, lambda q, c: (multiply(q, y), c)[1], 0)
+        lax.fori_loop(0, ys, lambda yy, c: (multiply(2 * yy, y), multiply(2 * yy + 1, y), c)[2], 0)
+
+    def gather_squares(j, total):
+        square_copy(j).wait()
+        return total + row_sq_recv[j]
+
+    total = lax.fori_loop(1, sps, gather_squares, row_sq[s])
+    mine = pl.ds(pl.multiple_of(s * rows, rows), rows)
+    visual = jnp.max(onehot[mine, :].astype(F32), axis=1, keepdims=True)
+    scale = as_column(lax.rsqrt(total / total_features + EPS))[:, :width]
+    scale = jnp.where(visual > 0.5, 1.0, scale)
 
     def place_tokens(p, side, yy):
         at = pl.ds(pl.multiple_of((yy * 2 + side) * rows, rows), rows)
@@ -308,27 +317,39 @@
         lax.fori_loop(1, ys + 1, lambda j, c: (place_tokens(p, core, lax.rem(y + j, ys)), c)[1], 0)
         pass_on(y, p)
 
-    def gather_squares(j, total):
-        square_copy(j).wait()
-        return total + row_sq_recv[j]
-
-    total = lax.fori_loop(1, sps, gather_squares, row_sq[s])
-    mine = pl.ds(pl.multiple_of(s * rows, rows), rows)
-    visual = jnp.max(onehot[mine, :].astype(F32), axis=1, keepdims=True)
-    scale = as_column(lax.rsqrt(total / total_features + EPS))[:, :width]
-    scale = jnp.where(visual > 0.5, 1.0, scale)
-    for p in range(pieces):
-        for yc in range(ys):
-            def add(j, sums):
-                y_copy(yc, p, j).wait()
-                return sums + y_recv[yc, p, j].astype(F32)
-
-            core_copy(yc, p, y).wait()
-            sums = part[yc, p, core, y].astype(F32) + core_recv[yc, p, y].astype(F32)
-            sums = lax.fori_loop(1, ys, add, sums)
-            first = yc * share + p * width
-            result[0, :, first:first + width] = (sums[0] * scale).astype(BF16)
-            result[1, :, first:first + width] = (sums[1] * scale).astype(BF16)
+    def finish(yc, p, index, first):
+        def add(j, sums):
+            y_copy(yc, p, j).wait()
+            return sums + y_recv[yc, p, j].astype(F32)
+
+        core_copy(yc, p, y).wait()
+        sums = part[yc, p, core, y].astype(F32) + core_recv[yc, p, y].astype(F32)
+        sums = lax.fori_loop(1, ys, add, sums)
+        columns = pl.ds(first, width)
+        held[0, :, columns] = (sums[0] * scale).astype(BF16)
+        held[1, :, columns] = (sums[1] * scale).astype(BF16)
+        if by_share:
+            result_copy(columns, index).start()
+
+    def result_copy(columns, index):
+        return pltpu.make_async_copy(held.at[:, :, columns], result.at[:, :, columns], result_sem.at[index])
+
+    for turn in range(ys):
+        for p in range(pieces):
+            if by_share:
+                yc = lax.rem(y + turn, ys)
+                finish(yc, p, turn * pieces + p, pl.multiple_of(yc * share + p * width, width))
+            else:
+                finish(turn, p, 0, turn * share + p * width)
+    if not by_share:
+        everything = pltpu.make_async_copy(held, result, result_sem.at[0])
+        everything.start()
+        everything.wait()
+    else:
+        for turn in range(ys):
+            for p in range(pieces):
+                first = pl.multiple_of(lax.rem(y + turn, ys) * share + p * width, width)
+                result_copy(pl.ds(first, width), turn * pieces + p).wait()
 
 
 def split(both, key_out, value_out, held, in_sem, out_sem):
@@ -372,7 +393,7 @@
         functools.partial(kernel, dims),
         out_shape=jax.ShapeDtypeStruct((2, rows, cols), BF16),
         in_specs=[smem, vmem, vmem] + [anywhere] * 5,
-        out_specs=vmem,
+        out_specs=anywhere,
         scratch_shapes=[
             pltpu.VMEM((tokens, raw), BF16),
             pltpu.VMEM((raw, features), BF16),
@@ -402,6 +423,7 @@
             dma((sps,)), dma((sps,)),
             dma((ys, pieces, ys)), dma((ys, pieces, ys)),
             dma((ys, pieces, ys)), dma((ys, pieces, ys)),
+            pltpu.VMEM((2, rows, cols), BF16), dma((ys * pieces,)),
         ] + [pltpu.VMEM((groups, pad, width), BF16)] * pieces,
         compiler_params=pltpu.CompilerParams(
             collective_id=0, has_side_effects=True, vmem_limit_bytes=60 * 1024 * 1024

time: 30.6 us -> 33.7 us (1.10)
  Pallas kernels: 29.7 us -> 32.8 us
    pallas_call x1, Pallas kernels: 27.9 us -> 31.1 us  [local(): pl.pallas_call(functools.partial(kernel, dims), out_shape=jax.ShapeDtypeS...]
where the time goes in v4:
time: 33.7 us; the launch traced here: 33.5 us
  Pallas kernels  32.8 us (97%)
  between operations  0.64 us (2%)
    pallas_call x1, Pallas kernels, local(): pl.pallas_call(functools.partial(kernel, dims), out_shape=jax.ShapeDtypeS...  31.1 us
    pallas_call x1, Pallas kernels, local(): pl.pallas_call(split, out_shape=[jax.ShapeDtypeStruct((rows, cols), BF16)...  1.77 us

profile of v4, /device:TPU:0, one launch (start us, length us, event | category | flops | bytes accessed | tf_op | source)
XLA Modules:
  0.0 33.5 jit_solution(10172307813553677989)
XLA Ops:
  0.6 31.1 %route_project.1.both = bf16[2,256,512]{2,1,0:T(8,128)(2,1)} custom-call(s32[2048]{0:T(1024)} %dest.1, s32[1,1024]{1,0:T(1,128)} %lay.1, f32[1,1024]{1,0:T(1,128)} %bitcast.1, bf16[256,1152]{1,0:T(8,128)(2,1)} %vis_hbm.1, bf16[1152,1024]{1,0:T(8,128)(2,1)} %proj_hbm.1, bf16[1024,1024]{1,0:T(8,128)(2,1)} %text_hbm.1, bf16[1024,512]{1,0:T(8,128)(2,1)} %key_hbm.1, ...), custom_call_target="tpu_custom_call" | custom-call | flops 5000000000 | bytes 8388608 | tf_op jit(solution)/shard_map/route_project/pallas_call | solution.py:392
  31.7 1.8 %split_result.1 = (bf16[256,512]{1,0:T(8,128)(2,1)}, bf16[256,512]{1,0:T(8,128)(2,1)}) custom-call(bf16[2,256,512]{2,1,0:T(8,128)(2,1)} %route_project.1.both), custom_call_target="tpu_custom_call" | custom-call | tf_op jit(solution)/shard_map/split_result/pallas_call | solution.py:434

commit v5 on v4

--- a/solution.py
+++ b/solution.py
@@ -63,6 +63,7 @@
         proj_copy(n).start()
     load_key = load(key_hbm, weight.at[0], 1)
     load_value = load(value_hbm, weight.at[1], 2)
+    load_text = load(text_hbm, text, 3)
 
     barrier = pltpu.get_barrier_semaphore()
 
@@ -97,15 +98,14 @@
 
     load_vis.wait()
 
-    squares = jnp.zeros((vis.shape[0], 1), F32)
-    for n in range(features // tile):
+    def project(n, total):
         proj_copy(n).wait()
-        if n == 0:
-            load_text = load(text_hbm, text, 3)
-        columns = pl.ds(n * tile, tile)
+        columns = pl.ds(pl.multiple_of(n * tile, tile), tile)
         block = jnp.dot(vis[...], proj[:, columns], preferred_element_type=F32).astype(BF16).astype(F32)
         tok[:, columns] = (block * gain[:, columns]).astype(BF16)
-        squares = squares + jnp.sum(block * block, axis=1, keepdims=True)
+        return total + jnp.sum(block * block, axis=1, keepdims=True)
+
+    squares = lax.fori_loop(0, features // tile, project, jnp.zeros((vis.shape[0], 1), F32))
     tok_sq[...] = as_row(squares)
     pl.semaphore_wait(barrier, groups - 1 + sps - 1)
 
@@ -224,15 +224,16 @@
         lax.fori_loop(1, ys, one, 0)
 
     def prepare(yy):
-        for side in range(2):
+        def one(side, carry):
             q = yy * 2 + side
             place(q)
-            if not by_share:
+            if by_share:
+                lax.fori_loop(1, ys, lambda j, c: (multiply(q, lax.rem(y + j, ys)), c)[1], 0)
+            else:
                 multiply_all(q)
-            elif ys == 2:
-                multiply(q, 1 - y)
-            else:
-                lax.fori_loop(1, ys, lambda j, c: (multiply(q, lax.rem(y + j, ys)), c)[1], 0)
+            return carry
+
+        lax.fori_loop(0, 2, one, 0)
 
         def send_share(j, carry):
             for p in range(pieces):
@@ -285,7 +286,7 @@
     lax.fori_loop(1, sps, lambda j, c: (square_copy(j).start(), c)[1], 0)
 
     if by_share:
-        lax.fori_loop(0, ys, lambda yy, c: (multiply(2 * yy, y), multiply(2 * yy + 1, y), c)[2], 0)
+        lax.fori_loop(0, sps, lambda q, c: (multiply(q, y), c)[1], 0)
 
     def gather_squares(j, total):
         square_copy(j).wait()

time: 33.7 us -> 33.7 us (level)
  no operation moved by 1% of the time
where the time goes in v5:
time: 33.7 us; the launch traced here: 33.5 us
  Pallas kernels  32.8 us (97%)
  between operations  0.64 us (2%)
    pallas_call x1, Pallas kernels, local(): pl.pallas_call(functools.partial(kernel, dims), out_shape=jax.ShapeDtypeS...  31.1 us
    pallas_call x1, Pallas kernels, local(): pl.pallas_call(split, out_shape=[jax.ShapeDtypeStruct((rows, cols), BF16)...  1.77 us

profile of v5, /device:TPU:0, one launch (start us, length us, event | category | flops | bytes accessed | tf_op | source)
XLA Modules:
  0.0 33.5 jit_solution(17258169837441235482)
XLA Ops:
  0.6 31.1 %route_project.1.both = bf16[2,256,512]{2,1,0:T(8,128)(2,1)} custom-call(s32[2048]{0:T(1024)} %dest.1, s32[1,1024]{1,0:T(1,128)} %lay.1, f32[1,1024]{1,0:T(1,128)} %bitcast.1, bf16[256,1152]{1,0:T(8,128)(2,1)} %vis_hbm.1, bf16[1152,1024]{1,0:T(8,128)(2,1)} %proj_hbm.1, bf16[1024,1024]{1,0:T(8,128)(2,1)} %text_hbm.1, bf16[1024,512]{1,0:T(8,128)(2,1)} %key_hbm.1, ...), custom_call_target="tpu_custom_call" | custom-call | flops 5000000000 | bytes 8388608 | tf_op jit(solution)/shard_map/route_project/pallas_call | solution.py:393
  31.7 1.8 %split_result.1 = (bf16[256,512]{1,0:T(8,128)(2,1)}, bf16[256,512]{1,0:T(8,128)(2,1)}) custom-call(bf16[2,256,512]{2,1,0:T(8,128)(2,1)} %route_project.1.both), custom_call_target="tpu_custom_call" | custom-call | tf_op jit(solution)/shard_map/split_result/pallas_call | solution.py:435
